TPU v7x, 32 devices: a whole 2x2x4 slice. The times are simulated.
32 devices in a mesh: slab: 4 (over z), brick: 8 (over y, x, core).
Axes of the slice: x: 2, y: 2, z: 4, core: 2. Of those that a mesh axis runs over, the one named last changes fastest.
Arguments:
- estimate: float32 [32, 512, 128], P('slab', 'brick'), may hold values from 0.5 to 2
- stored_data: float32 [8, 8, 6, 32, 16, 128], P('brick', None, None, 'slab'), may hold values from 0.5 to 2
- routes: int32 [8, 24], replicated, may hold values from 0 to 7, as said below
- offsets: int32 [6, 32], replicated, may hold values from -2 to 2
- depth_taps: float32 [6, 9], replicated, may hold values from 0.1 to 1
- row_taps: float32 [6, 5], replicated, may hold values from 0.1 to 1
- column_taps: float32 [6, 9], replicated, may hold values from 0.1 to 1
- background: float32 [6], replicated, may hold values from 0.2 to 0.6
Outputs:
- restored: float32 [32, 512, 128], P('slab', 'brick')
Inputs may be any that keep to these rules, and one draw needn't show every extreme that they name: routes[b, q] is the owner of block q % 4 of view q // 4 within device b's y-rows; an owner holds at most 6 blocks of one device's rows, and 2 owners hold 6 blocks of every device's rows.
All inputs are finite; a program needn't handle non-finite values.
Results may differ from a plain program's by a relative error of at most 0.00031.
Values may be sent and summed in bfloat16 or wider, within the bound.
A program may use at most 128 MiB of HBM per device.

v0:
```python
import jax
import jax.numpy as jnp
from jax import lax
from jax.sharding import PartitionSpec as P

V = 6
CX = 128
BY = 16
KB = 4
W = 4
RY = 2
RX = 4
ITERS = 2


def with_halo(cells, sides, width):
    for axis, dim in sides:
        count = lax.axis_size(axis)
        ends = count - 1
        head = lax.slice_in_dim(cells, 0, width, axis=dim)
        tail = lax.slice_in_dim(cells, cells.shape[dim] - width, cells.shape[dim], axis=dim)
        cells = jnp.concatenate(
            [
                lax.ppermute(tail, axis, [(i, (i + 1) % count) for i in range(ends)]),
                cells,
                lax.ppermute(head, axis, [((i + 1) % count, i) for i in range(ends)]),
            ],
            axis=dim,
        )
    return cells


def normalized(taps):
    return taps / jnp.sum(taps, axis=-1, keepdims=True)


def cross_matrix(column_kernel):
    row_index = jnp.arange(CX, dtype=jnp.int32)[:, None]
    col_index = jnp.arange(CX, dtype=jnp.int32)[None, :]
    lag_index = row_index - col_index + RX
    summed = jnp.zeros(column_kernel.shape[:-1] + (CX, CX), jnp.float32)
    for position in range(2 * RX + 1):
        summed = summed + column_kernel[..., position, None, None] * (lag_index == position).astype(
            jnp.float32
        )
    return summed.astype(jnp.bfloat16)


def slot_numbers(routes):
    width_count = routes.shape[1]
    same_owner = routes[:, :, None] == routes[:, None, :]
    earlier = (
        jnp.arange(width_count, dtype=jnp.int32)[None, :]
        < jnp.arange(width_count, dtype=jnp.int32)[:, None]
    )
    return jnp.sum((same_owner & earlier[None]).astype(jnp.int32), axis=2)


def pick_rows(table, views):
    chooser = (views[:, None] == jnp.arange(V, dtype=jnp.int32)[None, :]).astype(jnp.float32)
    expanded = chooser.reshape(chooser.shape + (1,) * (table.ndim - 1))
    return jnp.sum(expanded * table[None], axis=1)


def correct(windows, blocks, depth_kernel, row_kernel, matrices, floor_level):
    depth_cells = blocks.shape[1]
    across = jnp.einsum("szyx,sxw->szyw", windows, matrices, preferred_element_type=jnp.float32)
    row_blur = row_kernel[:, 0, None, None, None] * across[:, :, 0:BY]
    for position in range(1, 2 * RY + 1):
        row_blur = (
            row_blur
            + row_kernel[:, position, None, None, None] * across[:, :, position : position + BY]
        )
    blurred = depth_kernel[:, 0, None, None, None] * row_blur[:, 0:depth_cells]
    for position in range(1, 2 * W + 1):
        blurred = (
            blurred
            + depth_kernel[:, position, None, None, None]
            * row_blur[:, position : position + depth_cells]
        )
    ratio = blocks / (floor_level[:, None, None, None] + blurred)
    backward = jnp.einsum(
        "szyx,swx->szyw", ratio.astype(jnp.bfloat16), matrices, preferred_element_type=jnp.float32
    )
    row_back = 0.0
    for position in range(2 * RY + 1):
        widened = jnp.pad(backward, ((0, 0), (0, 0), (position, 2 * RY - position), (0, 0)))
        row_back = row_back + row_kernel[:, position, None, None, None] * widened
    depth_back = 0.0
    for position in range(2 * W + 1):
        widened = jnp.pad(row_back, ((0, 0), (position, 2 * W - position), (0, 0), (0, 0)))
        depth_back = depth_back + depth_kernel[:, position, None, None, None] * widened
    return depth_back


def fold_axis(padded, axis_number, inner):
    own_part = lax.slice_in_dim(padded, 2 * W, 2 * W + inner, axis=axis_number)
    upper_part = lax.slice_in_dim(padded, inner + 3 * W, inner + 4 * W, axis=axis_number)
    lower_part = lax.slice_in_dim(padded, 0, W, axis=axis_number)
    upper_widths = [(0, 0)] * padded.ndim
    lower_widths = [(0, 0)] * padded.ndim
    upper_widths[axis_number] = (inner - W, 0)
    lower_widths[axis_number] = (0, inner - W)
    return own_part + jnp.pad(upper_part, upper_widths) + jnp.pad(lower_part, lower_widths)


def local(estimate, stored_data, routes, offsets, depth_taps, row_taps, column_taps, background):
    brick_count = lax.axis_size("brick")
    brick_index = lax.axis_index("brick")
    depth_cells, height_cells, width_cells = estimate.shape
    block_total = routes.shape[1]
    capacity = stored_data.shape[2]
    slots_total = brick_count * capacity
    window_depth = depth_cells + 2 * W
    window_rows = BY + 2 * RY
    kernel_z = normalized(depth_taps)
    kernel_y = normalized(row_taps)
    kernel_x = normalized(column_taps)
    slots = slot_numbers(routes)
    my_routes = lax.dynamic_index_in_dim(routes, brick_index, 0, keepdims=False)
    my_slots = lax.dynamic_index_in_dim(slots, brick_index, 0, keepdims=False)
    slot_ids = my_routes * capacity + my_slots
    block_order = jnp.arange(block_total, dtype=jnp.int32)
    my_offsets = lax.dynamic_slice_in_dim(offsets, brick_index * KB, KB, 1).reshape(-1)
    starts = W + block_order % KB * BY + my_offsets - RY
    slot_mask = (routes[:, None, :] == brick_index) & (
        slots[:, None, :] == jnp.arange(capacity, dtype=jnp.int32)[None, :, None]
    )
    views = jnp.sum(
        slot_mask.astype(jnp.int32) * (block_order // KB)[None, None, :], axis=2
    ).reshape(-1)
    blocks = stored_data.reshape(slots_total, depth_cells, BY, width_cells)
    chooser = (jnp.arange(slots_total, dtype=jnp.int32)[:, None] == slot_ids[None, :]).astype(
        jnp.bfloat16
    )
    depth_kernel = pick_rows(kernel_z, views)
    row_kernel = pick_rows(kernel_y, views)
    matrices = cross_matrix(pick_rows(kernel_x, views))
    floor_level = pick_rows(background, views)
    for sweep in range(ITERS):
        rounded = estimate.astype(jnp.bfloat16)
        extended = with_halo(rounded, (("slab", 0), ("brick", 1)), W)
        windows = jax.vmap(
            lambda start_row: lax.dynamic_slice_in_dim(extended, start_row, window_rows, 1)
        )(starts)
        outgoing = jnp.dot(
            chooser, windows.reshape(block_total, -1), preferred_element_type=jnp.float32
        ).astype(jnp.bfloat16)
        outgoing = outgoing.reshape(brick_count, capacity, window_depth, window_rows, width_cells)
        incoming = lax.all_to_all(outgoing, "brick", split_axis=0, concat_axis=0, tiled=True)
        updates = correct(
            incoming.reshape(slots_total, window_depth, window_rows, width_cells),
            blocks,
            depth_kernel,
            row_kernel,
            matrices,
            floor_level,
        )
        returned = lax.all_to_all(
            updates.reshape(brick_count, capacity, window_depth, window_rows, width_cells),
            "brick",
            split_axis=0,
            concat_axis=0,
            tiled=True,
        )
        updates = jnp.take(
            returned.reshape(slots_total, window_depth, window_rows, width_cells), slot_ids, axis=0
        )

        def add_window(position, summed):
            start_row = starts[position]
            current = lax.dynamic_slice_in_dim(summed, start_row, window_rows, 1)
            return lax.dynamic_update_slice_in_dim(
                summed, current + updates[position], start_row, 1
            )

        summed = lax.fori_loop(
            0,
            block_total,
            add_window,
            jnp.zeros((window_depth, height_cells + 2 * W, width_cells), jnp.float32),
        )
        gathered = with_halo(summed, (("slab", 0), ("brick", 1)), W)
        folded = fold_axis(fold_axis(gathered, 0, depth_cells), 1, height_cells)
        estimate = estimate * (folded / V)
    return estimate


def solution(mesh):
    placed = (
        P("slab", "brick", None),
        P("brick", None, None, "slab", None, None),
        P(),
        P(),
        P(),
        P(),
        P(),
        P(),
    )
    return jax.shard_map(
        local, mesh=mesh, in_specs=placed, out_specs=P("slab", "brick", None), check_vma=False
    )
```

profile of v0, /device:TPU:4, one launch (start us, length us, event | category | flops | bytes accessed | tf_op | source)
XLA Modules:
  0.0 731.7 jit_solution(14130126039789229548)
XLA Ops:
  1.2 3.5 collective-permute-start
  7.2 3.6 collective-permute-done.1
  12.8 4.5 collective-permute-start.3
  19.9 2.0 copy.69
  21.9 3.0 reshape.291
  25.0 3.1 convolution_convert_fusion.1
  28.1 6.8 reshape.292
  34.9 5.3 copy.70
  40.2 5.2 all-to-all-start
  47.2 43.6 %all-to-all-done = bf16[8,6,16,20,128]{4,2,3,1,0:T(8,128)(2,1)} async-done(((bf16[8,6,16,20,128]{4,2,3,1,0:T(8,128)(2,1)}), bf16[8,6,16,20,128]{4,2,3,1,0:T(8,128)(2,1)}, u32[]{:S(2)}, u32[]{:S(2)}) %all-to-all-start) | async-done | bytes 3932192 | tf_op jit(solution)/shard_map/all_to_all | solution.py:150
  90.8 3.3 copy.71
  94.1 5.8 fusion.85
  99.9 22.0 %fusion.4 = f32[48,16,16,128]{3,2,1,0:T(8,128)} fusion(f32[48,16,20,128]{3,2,1,0:T(8,128)} %fusion.85, f32[48]{0:T(128)S(1)} %get-tuple-element.239, f32[48]{0:T(128)S(1)} %get-tuple-element.240, f32[48]{0:T(128)S(1)} %get-tuple-element.241, f32[48]{0:T(128)S(1)} %get-tuple-element.242, f32[48]{0:T(128)S(1)} %get-tuple-element.238), kind=kLoop, calls=%fused_computation.28 | loop fusion | flops 14155776 | bytes 37749696 | tf_op jit(solution)/shard_map/add | solution.py:71
  121.9 12.7 %fusion.28 = bf16[48,8,16,128]{3,2,1,0:T(8,128)(2,1)S(1)} fusion(f32[48,16,16,128]{3,2,1,0:T(8,128)} %fusion.4, f32[1,8,6,8,16,128]{5,4,3,2,1,0:T(8,128)S(1)} %copy-done.2, f32[48]{0:T(128)S(1)} %get-tuple-element.221, f32[48]{0:T(128)S(1)} %get-tuple-element.222, f32[48]{0:T(128)S(1)} %get-tuple-element.223, f32[48]{0:T(128)S(1)} %get-tuple-element.224, ...), kind=kLoop, calls=%fused_computation.77 | loop fusion | flops 15728640 | bytes 33032064 | tf_op jit(solution)/shard_map/convert_element_type | solution.py:83
  134.6 2.3 fusion.83
  136.9 4.6 multiply_add_fusion.3
  141.5 7.2 multiply_add_fusion.1
  148.6 4.7 copy.73
  153.4 5.8 all-to-all-start.1
  159.1 87.1 %all-to-all-done.1 = f32[8,6,16,20,128]{4,2,3,1,0:T(8,128)} async-done(((f32[8,6,16,20,128]{4,2,3,1,0:T(8,128)}), f32[8,6,16,20,128]{4,2,3,1,0:T(8,128)}, u32[]{:S(2)}, u32[]{:S(2)}) %all-to-all-start.1) | async-done | bytes 7864352 | tf_op jit(solution)/shard_map/all_to_all | solution.py:159
  246.2 5.9 gather_fusion.2
  252.1 4.6 broadcast_select_fusion.1
  256.8 92.8 %while.26 = (s32[]{:T(128)}, f32[16,72,128]{2,0,1:T(8,128)S(1)}, s32[24]{0:T(128)S(1)}, f32[24,16,20,128]{3,1,2,0:T(8,128)}, s32[]{:T(128)}, /*index=5*/s32[]{:T(128)}, s32[]{:T(128)}) while((s32[]{:T(128)}, f32[16,72,128]{2,0,1:T(8,128)S(1)}, s32[24]{0:T(128)S(1)}, f32[24,16,20,128]{3,1,2,0:T(8,128)}, s32[]{:T(128)}, /*index=5*/s32[]{:T(128)}, ...), condition=%wide.region_10.12_spmd, body=%wide.region_9.11_spmd.sunk | while | flops 40965 | bytes 1507463 | solution.py:177
  349.7 3.6 collective-permute-start.4
  355.9 4.4 collective-permute-done.5
  362.3 4.5 collective-permute-start.7
  369.2 3.5 collective-permute-start.8
  374.6 4.3 collective-permute-done.9
  380.8 4.5 collective-permute-start.11
  390.0 3.0 reshape.296
  393.0 3.1 convolution_convert_fusion
  396.1 6.8 reshape.297
  402.9 3.4 copy.80
  406.3 49.3 %all_to_all.20 = bf16[8,6,16,20,128]{4,2,3,1,0:T(8,128)(2,1)S(1)} all-to-all(bf16[8,6,16,20,128]{4,2,3,1,0:T(8,128)(2,1)S(1)} %copy.80), channel_id=1, replica_groups=mesh['slab'=4,'brick'=8] {'brick'}, dimensions={0} | all-to-all | bytes 7864320 | tf_op jit(solution)/shard_map/all_to_all | solution.py:150
  456.8 5.9 fusion.81
  462.6 22.0 %fusion = f32[48,16,16,128]{3,2,1,0:T(8,128)} fusion(f32[48,16,20,128]{3,2,1,0:T(8,128)} %fusion.81, f32[48]{0:T(128)S(1)} %get-tuple-element.239, f32[48]{0:T(128)S(1)} %get-tuple-element.240, f32[48]{0:T(128)S(1)} %get-tuple-element.241, f32[48]{0:T(128)S(1)} %get-tuple-element.242, f32[48]{0:T(128)S(1)} %get-tuple-element.238), kind=kLoop, calls=%fused_computation.19 | loop fusion | flops 14155776 | bytes 37749696 | tf_op jit(solution)/shard_map/add | solution.py:71
  484.6 12.7 %fusion.29 = bf16[48,8,16,128]{3,2,1,0:T(8,128)(2,1)S(1)} fusion(f32[48,16,16,128]{3,2,1,0:T(8,128)} %fusion, f32[1,8,6,8,16,128]{5,4,3,2,1,0:T(8,128)S(1)} %copy-done.3, f32[48]{0:T(128)S(1)} %get-tuple-element.221, f32[48]{0:T(128)S(1)} %get-tuple-element.222, f32[48]{0:T(128)S(1)} %get-tuple-element.223, f32[48]{0:T(128)S(1)} %get-tuple-element.224, ...), kind=kLoop, calls=%fused_computation.78 | loop fusion | flops 15728640 | bytes 33032064 | tf_op jit(solution)/shard_map/convert_element_type | solution.py:83
  497.3 2.3 fusion.79
  499.6 4.6 multiply_add_fusion.2
  504.2 7.3 multiply_add_fusion
  511.4 4.7 copy.82
  516.1 6.3 all-to-all-start.3
  522.4 87.1 %all-to-all-done.3 = f32[8,6,16,20,128]{4,2,3,1,0:T(8,128)} async-done(((f32[8,6,16,20,128]{4,2,3,1,0:T(8,128)}), f32[8,6,16,20,128]{4,2,3,1,0:T(8,128)}, u32[]{:S(2)}, u32[]{:S(2)}) %all-to-all-start.3) | async-done | bytes 7864352 | tf_op jit(solution)/shard_map/all_to_all | solution.py:159
  609.5 5.9 gather_fusion.3
  615.4 4.6 broadcast_select_fusion
  620.1 92.8 %while.27 = (s32[]{:T(128)}, f32[16,72,128]{2,0,1:T(8,128)S(1)}, s32[24]{0:T(128)S(1)}, f32[24,16,20,128]{3,1,2,0:T(8,128)}, s32[]{:T(128)}, /*index=5*/s32[]{:T(128)}, s32[]{:T(128)}) while((s32[]{:T(128)}, f32[16,72,128]{2,0,1:T(8,128)S(1)}, s32[24]{0:T(128)S(1)}, f32[24,16,20,128]{3,1,2,0:T(8,128)}, s32[]{:T(128)}, ...), condition=%wide.region_12.14_spmd, body=%wide.region_11.13_spmd.sunk | while | flops 40965 | bytes 1507463 | solution.py:177
  717.5 4.4 collective-permute-done.13
  723.9 4.5 collective-permute-start.15
  (346 shorter events, 120.4 us)
Async XLA Ops:
  0.0 6.0 copy-start
  1.2 6.1 collective-permute-start
  4.7 6.2 collective-permute-start.1
  10.9 7.2 collective-permute-start.2
  12.8 6.0 collective-permute-start.3
  40.2 5.3 copy-start.5
  40.2 5.7 copy-start.6
  40.2 6.0 copy-start.7
  40.2 6.2 copy-start.8
  40.2 6.5 copy-start.11
  40.2 50.6 %all-to-all-start = ((bf16[8,6,16,20,128]{4,2,3,1,0:T(8,128)(2,1)}), bf16[8,6,16,20,128]{4,2,3,1,0:T(8,128)(2,1)}, u32[]{:S(2)}, u32[]{:S(2)}) async-start(bf16[8,6,16,20,128]{4,2,3,1,0:T(8,128)(2,1)} %copy.70), calls=%async_computation | async-start | bytes 7864320 | tf_op jit(solution)/shard_map/all_to_all | solution.py:150
  99.9 22.0 %copy-start.2 = (f32[1,8,6,8,16,128]{5,4,3,2,1,0:T(8,128)S(1)}, f32[1,8,6,8,16,128]{5,4,3,2,1,0:T(8,128)}, u32[]{:S(2)}) copy-start(f32[1,8,6,8,16,128]{5,4,3,2,1,0:T(8,128)} %param.15) | copy-start | bytes 9437188
  153.4 92.8 %all-to-all-start.1 = ((f32[8,6,16,20,128]{4,2,3,1,0:T(8,128)}), f32[8,6,16,20,128]{4,2,3,1,0:T(8,128)}, u32[]{:S(2)}, u32[]{:S(2)}) async-start(f32[8,6,16,20,128]{4,2,3,1,0:T(8,128)} %copy.73), calls=%async_computation.1 | async-start | bytes 15728640 | tf_op jit(solution)/shard_map/all_to_all | solution.py:159
  349.6 19.1 %copy-start.10 = (pred[8]{0:T(512)(128)(4,1)S(1)}, pred[8]{0:T(512)(128)(4,1)}, u32[]{:S(2)}) copy-start(pred[8]{0:T(512)(128)(4,1)} %constant.151.clone.1) | copy-start | bytes 28
  349.6 19.4 %copy-start.4 = (f32[8,64,128]{2,1,0:T(8,128)S(1)}, f32[8,64,128]{2,1,0:T(8,128)}, u32[]{:S(2)}) copy-start(f32[8,64,128]{2,1,0:T(8,128)} %param.14) | copy-start | bytes 786436
  349.6 19.4 %copy-start.9 = (pred[64]{0:T(512)(128)(4,1)S(1)}, pred[64]{0:T(512)(128)(4,1)}, u32[]{:S(2)}) copy-start(pred[64]{0:T(512)(128)(4,1)} %constant.152.clone.1) | copy-start | bytes 196
  349.7 6.3 collective-permute-start.4
  353.3 7.0 collective-permute-start.5
  360.4 6.5 collective-permute-start.6
  362.3 6.3 collective-permute-start.7
  369.2 5.4 collective-permute-start.8
  372.7 6.2 collective-permute-start.9
  378.9 6.5 collective-permute-start.10
  380.8 6.0 collective-permute-start.11
  462.6 22.0 %copy-start.3 = (f32[1,8,6,8,16,128]{5,4,3,2,1,0:T(8,128)S(1)}, f32[1,8,6,8,16,128]{5,4,3,2,1,0:T(8,128)}, u32[]{:S(2)}) copy-start(f32[1,8,6,8,16,128]{5,4,3,2,1,0:T(8,128)} %param.15) | copy-start | bytes 9437188
  516.1 93.4 %all-to-all-start.3 = ((f32[8,6,16,20,128]{4,2,3,1,0:T(8,128)}), f32[8,6,16,20,128]{4,2,3,1,0:T(8,128)}, u32[]{:S(2)}, u32[]{:S(2)}) async-start(f32[8,6,16,20,128]{4,2,3,1,0:T(8,128)} %copy.82), calls=%async_computation.3 | async-start | bytes 15728640 | tf_op jit(solution)/shard_map/all_to_all | solution.py:159
  712.9 18.5 %copy-start.1 = (s32[6,32]{1,0:T(8,128)S(1)}, s32[6,32]{1,0:T(8,128)}, u32[]{:S(2)}) copy-start(s32[6,32]{1,0:T(8,128)} %param.17) | copy-start | bytes 2308
  712.9 4.6 collective-permute-start.12
  714.9 7.0 collective-permute-start.13
  721.9 6.5 collective-permute-start.14
  723.9 6.3 collective-permute-start.15
where the time goes:
time: 742 us; the launch traced here: 732 us
  waiting for transfers between devices  243 us (33%)
  local copies, waits for them, and re-layouts  143 us (19%)
  other arithmetic  111 us (15%)
  loops' own time  101 us (14%)
  starting transfers between devices  60.7 us (8%)
  blocking collectives  49.3 us (7%)
  matrix products  22.5 us (3%)
    all_to_all x2, waiting for transfers between devices, local(): lax.all_to_all(updates.reshape(brick_count, capacity, window_depth, windo...  174 us
    another operation x2, loops' own time, local(): lax.fori_loop(0, block_total, add_window, jnp.zeros((window_depth, height...  101 us
    all_to_all x1, blocking collectives, local(): lax.all_to_all(outgoing, 'brick', split_axis=0, concat_axis=0, tiled=True)  49.3 us
    dynamic_slice x48, local copies, waits for them, and re-layouts, add_window(): updates[position]  44.8 us
    add x2, other arithmetic, correct(): row_blur + row_kernel[:, position, None, None, None] * across[:, :, posit...  43.9 us
    all_to_all x1, waiting for transfers between devices, local(): lax.all_to_all(outgoing, 'brick', split_axis=0, concat_axis=0, tiled=True)  43.6 us
    dynamic_slice x48, local copies, waits for them, and re-layouts, add_window(): start_row = starts[position]  32 us
    convert_element_type x2, other arithmetic, correct(): ratio.astype(jnp.bfloat16)  25.3 us
  transfers between devices with their start and end apart: 19, of which 14 were waited for; matrix products, arithmetic and copies ran while one was open for 0% of the time, Pallas kernels for 0%

commit v1 on v0

v1 whole, which is shorter than its diff:
```python
import functools

import jax
import jax.numpy as jnp
from jax import lax
from jax.experimental import pallas as pl
from jax.experimental.pallas import tpu as pltpu
from jax.sharding import PartitionSpec as P

V = 6
CX = 128
BY = 16
KB = 4
W = 4
RY = 2
RX = 4
ITERS = 2
TZ = 2 * W + 1
TY = 2 * RY + 1
TX = 2 * RX + 1
MIDDLE = 1.25
SCALE = 43680.0
DIRECTIONS = [(dz, db) for dz in (-1, 0, 1) for db in (-1, 0, 1) if (dz, db) != (0, 0)]
MESH = pl.DeviceIdType.MESH


def kernel(
    slabs,
    bricks,
    routes,
    offsets,
    depth_taps,
    row_taps,
    column_taps,
    background,
    estimate,
    stored,
    restored,
    staged,
    coded,
    received,
    slots,
    rounded,
    extended,
    zblur,
    back,
    spread,
    correction,
    total,
    forward,
    backward,
    scales,
    halos,
    returns,
    load_sem,
    data_send,
    data_recv,
    halo_send,
    halo_recv,
    return_send,
    return_recv,
):
    slab = lax.axis_index("slab")
    brick = lax.axis_index("brick")
    capacity = stored.shape[1]
    depth, height, _ = estimate.shape
    padded = height + 2 * W
    tiles = padded // 8

    def load_copy(target):
        return pltpu.make_async_copy(stored.at[target], staged.at[target], load_sem.at[target])

    for step in range(bricks):
        load_copy(lax.rem(brick + step, bricks)).start()

    def present(dz, db):
        there_slab = slab + dz
        there_brick = brick + db
        return (
            (there_slab >= 0) & (there_slab < slabs) & (there_brick >= 0) & (there_brick < bricks)
        )

    for buffer in tuple(halos) + tuple(returns):
        buffer[...] = jnp.zeros_like(buffer)

    barrier = pltpu.get_barrier_semaphore()
    for step in range(1, bricks):
        pl.semaphore_signal(
            barrier,
            inc=1,
            device_id=(slab, lax.rem(brick + step, bricks)),
            device_id_type=MESH,
        )
    expected = jnp.int32(bricks - 1)
    for dz, db in DIRECTIONS:
        if dz == 0:
            continue

        @pl.when(present(dz, db))
        def _():
            pl.semaphore_signal(
                barrier, inc=1, device_id=(slab + dz, brick + db), device_id_type=MESH
            )

        expected = expected + present(dz, db).astype(jnp.int32)
    estimate_now = estimate[...]
    rounded[0] = estimate_now.astype(jnp.bfloat16)
    pl.semaphore_wait(barrier, expected)

    def halo_copy(sweep, index):
        dz, db = DIRECTIONS[index]
        planes = {-1: pl.ds(0, W), 0: pl.ds(0, depth), 1: pl.ds(depth - W, W)}[dz]
        rows = {-1: pl.ds(0, 16), 0: pl.ds(0, height), 1: pl.ds(height - 16, 16)}[db]
        return pltpu.make_async_remote_copy(
            src_ref=rounded.at[sweep, planes, rows],
            dst_ref=halos[index].at[sweep],
            send_sem=halo_send.at[sweep, index],
            recv_sem=halo_recv.at[sweep, index],
            device_id=(slab + dz, brick + db),
            device_id_type=MESH,
        )

    def return_copy(sweep, index):
        dz, db = DIRECTIONS[index]
        planes = {-1: pl.ds(0, W), 0: pl.ds(W, depth), 1: pl.ds(depth + W, W)}[dz]
        rows = {-1: pl.ds(0, 8), 0: pl.ds(0, padded), 1: pl.ds(padded - 8, 8)}[db]
        return pltpu.make_async_remote_copy(
            src_ref=correction.at[sweep, planes, rows],
            dst_ref=returns[index].at[sweep],
            send_sem=return_send.at[sweep, index],
            recv_sem=return_recv.at[sweep, index],
            device_id=(slab + dz, brick + db),
            device_id_type=MESH,
        )

    def send_all(copy, sweep):
        for index, (dz, db) in enumerate(DIRECTIONS):

            @pl.when(present(dz, db))
            def _():
                copy(sweep, index).start()

    def receive_all(copy, sweep):
        for index, (dz, db) in enumerate(DIRECTIONS):

            @pl.when(present(-dz, -db))
            def _():
                copy(sweep, index).wait_recv()

    def sent_all(copy, sweep):
        for index, (dz, db) in enumerate(DIRECTIONS):

            @pl.when(present(dz, db))
            def _():
                copy(sweep, index).wait_send()

    def data_copy(target, source):
        return pltpu.make_async_remote_copy(
            src_ref=coded.at[target],
            dst_ref=received.at[brick],
            send_sem=data_send.at[target],
            recv_sem=data_recv.at[source],
            device_id=(slab, target),
            device_id_type=MESH,
        )

    def encode(cells):
        return jnp.round((cells - MIDDLE) * SCALE).astype(jnp.int32).astype(jnp.int16)

    send_all(halo_copy, 0)

    def send_step(step, carry):
        target = lax.rem(brick + step, bricks)
        load_copy(target).wait()

        def code_slot(slot, inner):
            coded[target, slot] = encode(staged[target, slot])
            return inner

        lax.fori_loop(0, capacity, code_slot, 0)
        data_copy(target, brick).start()
        return carry

    lax.fori_loop(1, bricks, send_step, 0)
    load_copy(brick).wait()

    def code_own(slot, carry):
        received[brick, slot] = encode(staged[brick, slot])
        return carry

    lax.fori_loop(0, capacity, code_own, 0)

    def number_slots(position, carry):
        owner = routes[brick, position]
        count = jnp.int32(0)
        for other in range(V * KB):
            same = (routes[brick, other] == owner) & (other < position)
            count = count + jnp.where(same, 1, 0)
        slots[position] = jnp.minimum(count, capacity - 1)
        return carry

    lax.fori_loop(0, V * KB, number_slots, 0)

    row_index = lax.broadcasted_iota(jnp.int32, (CX, CX), 0)
    col_index = lax.broadcasted_iota(jnp.int32, (CX, CX), 1)

    def build_view(view, carry):
        sum_x = column_taps[view, 0]
        for position in range(1, TX):
            sum_x = sum_x + column_taps[view, position]
        sum_y = row_taps[view, 0]
        for position in range(1, TY):
            sum_y = sum_y + row_taps[view, position]
        sum_z = depth_taps[view, 0]
        for position in range(1, TZ):
            sum_z = sum_z + depth_taps[view, position]
        ones = jnp.ones((8, CX), jnp.float32)
        scales[view] = ones / (ones * (sum_y * sum_z))
        lag = row_index - col_index + RX
        matrix = jnp.zeros((CX, CX), jnp.float32)
        flipped = jnp.zeros((CX, CX), jnp.float32)
        bottom = jnp.full((1, CX), sum_x, jnp.float32)
        for position in range(TX):
            tap = jnp.full((1, CX), column_taps[view, position], jnp.float32) / bottom
            matrix = jnp.where(lag == position, tap, matrix)
            flipped = jnp.where(lag == 2 * RX - position, tap, flipped)
        matrix = matrix.astype(jnp.bfloat16)
        forward[view, 0:CX] = matrix
        forward[view, CX : 2 * CX] = matrix
        backward[view] = flipped.astype(jnp.bfloat16)
        return carry

    lax.fori_loop(0, V, build_view, 0)

    def clear(position, carry):
        back[position, :, 0:8] = jnp.zeros((depth, 8, CX), jnp.float32)
        back[position, :, 8 + BY : 16 + BY] = jnp.zeros((depth, 8, CX), jnp.float32)
        return carry

    lax.fori_loop(0, V * KB, clear, 0)

    for sweep in range(ITERS):
        if sweep > 0:
            rounded[sweep] = estimate_now.astype(jnp.bfloat16)
            send_all(halo_copy, sweep)
        extended[W : W + depth, W : W + height] = rounded[sweep].astype(jnp.float32)
        receive_all(halo_copy, sweep)
        for index, (dz, db) in enumerate(DIRECTIONS):
            planes = {1: (0, W), 0: (W, W + depth), -1: (W + depth, 2 * W + depth)}[dz]
            rows = {1: (0, W), 0: (W, W + height), -1: (W + height, padded)}[db]
            taken = {1: (16 - W, 16), 0: (0, height), -1: (0, W)}[db]
            block = halos[index][sweep].astype(jnp.float32)
            extended[planes[0] : planes[1], rows[0] : rows[1]] = block[:, taken[0] : taken[1]]

        def blur_tile(tile, carry):
            start = pl.multiple_of(tile * 8, 8)
            planes = [extended[z, pl.ds(start, 8)] for z in range(depth + 2 * W)]
            for view in range(V):
                taps = [depth_taps[view, position] for position in range(TZ)]
                for z in range(depth):
                    value = taps[0] * planes[z]
                    for position in range(1, TZ):
                        value = value + taps[position] * planes[z + position]
                    zblur[view, z, pl.ds(start, 8)] = value
            return carry

        lax.fori_loop(0, tiles, blur_tile, 0)

        if sweep == 0:

            def receive_step(step, carry):
                source = lax.rem(brick + step, bricks)
                data_copy(source, source).wait_recv()
                return carry

            lax.fori_loop(1, bricks, receive_step, 0)

        def block_step(position, carry):
            view = position // KB
            piece = position % KB
            shift = offsets[view, brick * KB + piece]
            first = piece * BY + W - RY + shift
            blurred = row_taps[view, 0] * zblur[view, :, pl.ds(first, BY)]
            for tap in range(1, TY):
                blurred = blurred + row_taps[view, tap] * zblur[view, :, pl.ds(first + tap, BY)]
            blurred = blurred.reshape(depth * BY, CX)
            high = blurred.astype(jnp.bfloat16)
            low = (blurred - high.astype(jnp.float32)).astype(jnp.bfloat16)
            factor = scales[view, 0:1]
            blurred = factor * jnp.dot(
                jnp.concatenate([high, low], axis=1),
                forward[view],
                preferred_element_type=jnp.float32,
            )
            code = received[routes[brick, position], slots[position]].astype(jnp.int32)
            data = code.astype(jnp.float32) * (1.0 / SCALE) + MIDDLE
            ratio = data.reshape(depth * BY, CX) / (background[view] + blurred)
            result = factor * jnp.dot(
                ratio.astype(jnp.bfloat16), backward[view], preferred_element_type=jnp.float32
            )
            back[position, :, 8 : 8 + BY] = result.reshape(depth, BY, CX)
            return carry

        lax.fori_loop(0, V * KB, block_step, 0)

        def spread_view(view, carry):
            edge = None
            for piece in range(KB):
                position = view * KB + piece
                shift = offsets[view, brick * KB + piece]
                value = None
                for tap in range(TY):
                    term = row_taps[view, tap] * back[
                        position, :, pl.ds(W - shift - (tap - RY), BY + 2 * W)
                    ]
                    value = term if value is None else value + term
                top = value[:, 0:8]
                if edge is not None:
                    top = top + edge
                spread[view, :, piece * BY : piece * BY + 8] = top
                spread[view, :, piece * BY + 8 : piece * BY + 16] = value[:, 8:16]
                edge = value[:, 16:24]
            spread[view, :, KB * BY : KB * BY + 8] = edge
            return carry

        lax.fori_loop(0, V, spread_view, 0)

        def deep_tile(tile, carry):
            start = pl.multiple_of(tile * 8, 8)
            sums = [None] * (depth + 2 * W)
            for view in range(V):
                taps = [depth_taps[view, position] for position in range(TZ)]
                for z in range(depth):
                    plane = spread[view, z, pl.ds(start, 8)]
                    for position in range(TZ):
                        term = taps[position] * plane
                        old = sums[z + position]
                        sums[z + position] = term if old is None else old + term
            for z in range(depth + 2 * W):
                correction[sweep, z, pl.ds(start, 8)] = sums[z]
            return carry

        lax.fori_loop(0, tiles, deep_tile, 0)

        send_all(return_copy, sweep)
        total[...] = correction[sweep, W : W + depth, W : W + height]
        receive_all(return_copy, sweep)
        for index, (dz, db) in enumerate(DIRECTIONS):
            planes = {1: (0, W), 0: (0, depth), -1: (depth - W, depth)}[dz]
            rows = {1: (0, W), 0: (0, height), -1: (height - W, height)}[db]
            taken = {1: (8 - W, 8), 0: (W, W + height), -1: (0, W)}[db]
            total[planes[0] : planes[1], rows[0] : rows[1]] += returns[index][
                sweep, :, taken[0] : taken[1]
            ]
        if sweep + 1 < ITERS:
            estimate_now = estimate_now * (total[...] / V)
        else:
            restored[...] = estimate_now * (total[...] / V)

    for sweep in range(ITERS):
        sent_all(halo_copy, sweep)
        sent_all(return_copy, sweep)

    def sent_step(step, carry):
        data_copy(lax.rem(brick + step, bricks), brick).wait_send()
        return carry

    lax.fori_loop(1, bricks, sent_step, 0)


def local(slabs, bricks, estimate, stored_data, routes, offsets, depth_taps, row_taps, column_taps, background):
    depth, height, width = estimate.shape
    stored = stored_data.reshape(stored_data.shape[1:])
    capacity = stored.shape[1]
    padded = height + 2 * W
    halo_planes = {-1: W, 0: depth, 1: W}
    halo_rows = {-1: 16, 0: height, 1: 16}
    return_rows = {-1: 8, 0: padded, 1: 8}
    smem = pl.BlockSpec(memory_space=pltpu.SMEM)
    vmem = pl.BlockSpec(memory_space=pltpu.VMEM)
    count = len(DIRECTIONS)
    return pl.pallas_call(
        functools.partial(kernel, slabs, bricks),
        out_shape=jax.ShapeDtypeStruct((depth, height, width), jnp.float32),
        in_specs=[smem] * 6 + [vmem, pl.BlockSpec(memory_space=pl.ANY)],
        out_specs=vmem,
        scratch_shapes=[
            pltpu.VMEM((bricks, capacity, depth, BY, width), jnp.float32),
            pltpu.VMEM((bricks, capacity, depth, BY, width), jnp.int16),
            pltpu.VMEM((bricks, capacity, depth, BY, width), jnp.int16),
            pltpu.SMEM((V * KB,), jnp.int32),
            pltpu.VMEM((ITERS, depth, height, width), jnp.bfloat16),
            pltpu.VMEM((depth + 2 * W, padded, width), jnp.float32),
            pltpu.VMEM((V, depth, padded, width), jnp.float32),
            pltpu.VMEM((V * KB, depth, BY + 16, width), jnp.float32),
            pltpu.VMEM((V, depth, padded, width), jnp.float32),
            pltpu.VMEM((ITERS, depth + 2 * W, padded, width), jnp.float32),
            pltpu.VMEM((depth, height, width), jnp.float32),
            pltpu.VMEM((V, 2 * CX, CX), jnp.bfloat16),
            pltpu.VMEM((V, CX, CX), jnp.bfloat16),
            pltpu.VMEM((V, 8, CX), jnp.float32),
            [
                pltpu.VMEM((ITERS, halo_planes[dz], halo_rows[db], width), jnp.bfloat16)
                for dz, db in DIRECTIONS
            ],
            [
                pltpu.VMEM((ITERS, halo_planes[dz], return_rows[db], width), jnp.float32)
                for dz, db in DIRECTIONS
            ],
            pltpu.SemaphoreType.DMA((bricks,)),
            pltpu.SemaphoreType.DMA((bricks,)),
            pltpu.SemaphoreType.DMA((bricks,)),
            pltpu.SemaphoreType.DMA((ITERS, count)),
            pltpu.SemaphoreType.DMA((ITERS, count)),
            pltpu.SemaphoreType.DMA((ITERS, count)),
            pltpu.SemaphoreType.DMA((ITERS, count)),
        ],
        compiler_params=pltpu.CompilerParams(
            collective_id=0, has_side_effects=True, vmem_limit_bytes=48 * 2**20
        ),
    )(routes, offsets, depth_taps, row_taps, column_taps, background, estimate, stored)


def solution(mesh):
    placed = (
        P("slab", "brick", None),
        P("brick", None, None, "slab", None, None),
        P(),
        P(),
        P(),
        P(),
        P(),
        P(),
    )
    return jax.shard_map(
        functools.partial(local, mesh.shape["slab"], mesh.shape["brick"]),
        mesh=mesh,
        in_specs=placed,
        out_specs=P("slab", "brick", None),
        check_vma=False,
    )
```

time: 742 us -> 69.7 us (0.09); the launches traced: 732 us -> 69.4 us
  waiting for transfers between devices: 243 us -> 0 us
  local copies, waits for them, and re-layouts: 143 us -> 7.63 us
  other arithmetic: 111 us -> 0 us
  loops' own time: 101 us -> 0 us
  Pallas kernels: 0 us -> 61.7 us
  starting transfers between devices: 60.7 us -> 0 us
  blocking collectives: 49.3 us -> 0 us
  matrix products: 22.5 us -> 0 us
    all_to_all x3 -> x0, waiting for transfers between devices: 218 us -> none  [the longest x2 174 us: local(): lax.all_to_all(updates.reshape(brick_count, capacity, window_depth, windo...]
    another operation x2 -> x0, loops' own time: 101 us -> none  [local(): lax.fori_loop(0, block_total, add_window, jnp.zeros((window_depth, height...]
    dynamic_slice x145 -> x0, local copies, waits for them, and re-layouts: 77.7 us -> none  [the longest x48 44.8 us: add_window(): updates[position]]
    add x56 -> x0, other arithmetic: 72.7 us -> none  [the longest x2 43.9 us: correct(): row_blur + row_kernel[:, position, None, None, None] * across[:, :, posit...]
    pallas_call x0 -> x1, Pallas kernels: none -> 61.7 us  [local(): pl.pallas_call(functools.partial(kernel, slabs, bricks), out_shape=jax.Sh...]
    all_to_all x1 -> x0, blocking collectives: 49.3 us -> none  [local(): lax.all_to_all(outgoing, 'brick', split_axis=0, concat_axis=0, tiled=True)]
    ppermute x16 -> x0, starting transfers between devices: 43.5 us -> none  [the longest x8 23.3 us: with_halo(): lax.ppermute(head, axis, [((i + 1) % count, i) for i in range(ends)])]
    reshape x10 -> x0, local copies, waits for them, and re-layouts: 37.9 us -> none  [the longest x4 22.2 us: local(): outgoing.reshape(brick_count, capacity, window_depth, window_rows, width_...]
  transfers between devices with their start and end apart: 19 -> 0, of which waited for: 14 -> 0; matrix products, arithmetic and copies ran while one was open for 0% -> 0% of each run, Pallas kernels for 0% -> 0%
where the time goes in v1:
time: 69.7 us; the launch traced here: 69.4 us
  Pallas kernels  61.7 us (89%)
  local copies, waits for them, and re-layouts  7.63 us (11%)
    pallas_call x1, Pallas kernels, local(): pl.pallas_call(functools.partial(kernel, slabs, bricks), out_shape=jax.Sh...  61.7 us
    unnamed x17, local copies, waits for them, and re-layouts  7.63 us

profile of v1, /device:TPU:4, one launch (start us, length us, event | category | flops | bytes accessed | tf_op | source)
XLA Modules:
  0.0 69.4 jit_solution(5867113813407121844)
XLA Ops:
  0.0 0.0 copy-start
  0.0 1.9 %copy-done = f32[1,8,6,8,16,128]{5,4,3,2,1,0:T(8,128)S(1)} copy-done((f32[1,8,6,8,16,128]{5,4,3,2,1,0:T(8,128)S(1)}, f32[1,8,6,8,16,128]{5,4,3,2,1,0:T(8,128)}, u32[]{:S(2)}) %copy-start) | copy-done | bytes 3145752
  1.9 0.0 copy-start.1
  1.9 0.9 %copy-done.1 = f32[8,64,128]{2,1,0:T(8,128)S(1)} copy-done((f32[8,64,128]{2,1,0:T(8,128)S(1)}, f32[8,64,128]{2,1,0:T(8,128)}, u32[]{:S(2)}) %copy-start.1) | copy-done | bytes 262168
  2.8 0.0 copy-start.2
  2.8 0.7 copy-done.2
  3.5 0.0 copy-start.3
  3.5 0.7 copy-done.3
  4.2 0.0 copy-start.4
  4.2 0.7 copy-done.4
  4.9 0.0 copy-start.5
  4.9 0.7 copy-done.5
  5.6 0.0 copy-start.6
  5.6 0.7 copy-done.6
  6.3 0.0 copy-start.7
  6.3 0.7 copy-done.7
  6.9 61.7 %shard_map.82 = f32[8,64,128]{2,1,0:T(8,128)S(1)} custom-call(s32[8,24]{1,0:T(8,128)S(1)} %copy-done.2, s32[6,32]{1,0:T(8,128)S(1)} %copy-done.3, f32[6,9]{1,0:T(8,128)S(1)} %copy-done.4, f32[6,5]{1,0:T(8,128)S(1)} %copy-done.5, f32[6,9]{1,0:T(8,128)S(1)} %copy-done.6, f32[6]{0:T(128)S(1)} %copy-done.7, f32[8,64,128]{2,1,0:T(8,128)S(1)} %copy-done.1, ...), custom_call_target="tpu_custom_call" | custom-call | tf_op jit(solution)/shard_map/pallas_call | solution.py:382
  68.7 0.7 %copy.10 = f32[8,64,128]{2,1,0:T(8,128)} copy(f32[8,64,128]{2,1,0:T(8,128)S(1)} %shard_map.82) | data formatting | bytes 524288
Async XLA Ops:
  0.0 1.9 %copy-start = (f32[1,8,6,8,16,128]{5,4,3,2,1,0:T(8,128)S(1)}, f32[1,8,6,8,16,128]{5,4,3,2,1,0:T(8,128)}, u32[]{:S(2)}) copy-start(f32[1,8,6,8,16,128]{5,4,3,2,1,0:T(8,128)} %param.9) | copy-start | bytes 9437188
  1.9 0.9 %copy-start.1 = (f32[8,64,128]{2,1,0:T(8,128)S(1)}, f32[8,64,128]{2,1,0:T(8,128)}, u32[]{:S(2)}) copy-start(f32[8,64,128]{2,1,0:T(8,128)} %estimate.1) | copy-start | bytes 786436
  2.8 0.7 copy-start.2
  3.5 0.7 copy-start.3
  4.2 0.7 copy-start.4
  4.9 0.7 copy-start.5
  5.6 0.7 copy-start.6
  6.3 0.7 copy-start.7

commit v2 on v1

--- a/solution.py
+++ b/solution.py
@@ -27,6 +27,15 @@
 def kernel(
     slabs,
     bricks,
+    routes_in,
+    offsets_in,
+    depth_in,
+    row_in,
+    column_in,
+    background_in,
+    estimate_in,
+    stored,
+    restored,
     routes,
     offsets,
     depth_taps,
@@ -34,8 +43,7 @@
     column_taps,
     background,
     estimate,
-    stored,
-    restored,
+    small_sem,
     staged,
     coded,
     received,
@@ -43,6 +51,7 @@
     rounded,
     extended,
     zblur,
+    level,
     back,
     spread,
     correction,
@@ -70,7 +79,23 @@
     def load_copy(target):
         return pltpu.make_async_copy(stored.at[target], staged.at[target], load_sem.at[target])
 
-    for step in range(bricks):
+    small = [
+        pltpu.make_async_copy(source, target, small_sem.at[index])
+        for index, (source, target) in enumerate(
+            [
+                (estimate_in, estimate),
+                (routes_in, routes),
+                (offsets_in, offsets),
+                (depth_in, depth_taps),
+                (row_in, row_taps),
+                (column_in, column_taps),
+                (background_in, background),
+            ]
+        )
+    ]
+    for copy in small:
+        copy.start()
+    for step in range(1, bricks + 1):
         load_copy(lax.rem(brick + step, bricks)).start()
 
     def present(dz, db):
@@ -103,6 +128,7 @@
             )
 
         expected = expected + present(dz, db).astype(jnp.int32)
+    small[0].wait()
     estimate_now = estimate[...]
     rounded[0] = estimate_now.astype(jnp.bfloat16)
     pl.semaphore_wait(barrier, expected)
@@ -189,6 +215,9 @@
         return carry
 
     lax.fori_loop(0, capacity, code_own, 0)
+
+    for copy in small[1:]:
+        copy.wait()
 
     def number_slots(position, carry):
         owner = routes[brick, position]
@@ -266,6 +295,27 @@
 
         lax.fori_loop(0, tiles, blur_tile, 0)
 
+        def forward_view(view, carry):
+            parts = []
+            for piece in range(KB):
+                first = piece * BY + W - RY + offsets[view, brick * KB + piece]
+                part = row_taps[view, 0] * zblur[view, :, pl.ds(first, BY)]
+                for tap in range(1, TY):
+                    part = part + row_taps[view, tap] * zblur[view, :, pl.ds(first + tap, BY)]
+                parts.append(part.reshape(depth * BY, CX))
+            blurred = jnp.concatenate(parts, axis=0)
+            high = blurred.astype(jnp.bfloat16)
+            low = (blurred - high.astype(jnp.float32)).astype(jnp.bfloat16)
+            blurred = jnp.dot(
+                jnp.concatenate([high, low], axis=1),
+                forward[view],
+                preferred_element_type=jnp.float32,
+            )
+            level[view] = background[view] + scales[view, 0:1] * blurred
+            return carry
+
+        lax.fori_loop(0, V, forward_view, 0)
+
         if sweep == 0:
 
             def receive_step(step, carry):
@@ -275,33 +325,23 @@
 
             lax.fori_loop(1, bricks, receive_step, 0)
 
-        def block_step(position, carry):
-            view = position // KB
-            piece = position % KB
-            shift = offsets[view, brick * KB + piece]
-            first = piece * BY + W - RY + shift
-            blurred = row_taps[view, 0] * zblur[view, :, pl.ds(first, BY)]
-            for tap in range(1, TY):
-                blurred = blurred + row_taps[view, tap] * zblur[view, :, pl.ds(first + tap, BY)]
-            blurred = blurred.reshape(depth * BY, CX)
-            high = blurred.astype(jnp.bfloat16)
-            low = (blurred - high.astype(jnp.float32)).astype(jnp.bfloat16)
-            factor = scales[view, 0:1]
-            blurred = factor * jnp.dot(
-                jnp.concatenate([high, low], axis=1),
-                forward[view],
-                preferred_element_type=jnp.float32,
-            )
-            code = received[routes[brick, position], slots[position]].astype(jnp.int32)
-            data = code.astype(jnp.float32) * (1.0 / SCALE) + MIDDLE
-            ratio = data.reshape(depth * BY, CX) / (background[view] + blurred)
-            result = factor * jnp.dot(
+        def backward_view(view, carry):
+            codes = []
+            for piece in range(KB):
+                position = view * KB + piece
+                code = received[routes[brick, position], slots[position]].astype(jnp.int32)
+                codes.append(code.astype(jnp.float32).reshape(depth * BY, CX))
+            data = jnp.concatenate(codes, axis=0) * (1.0 / SCALE) + MIDDLE
+            ratio = data / level[view]
+            result = scales[view, 0:1] * jnp.dot(
                 ratio.astype(jnp.bfloat16), backward[view], preferred_element_type=jnp.float32
             )
-            back[position, :, 8 : 8 + BY] = result.reshape(depth, BY, CX)
+            result = result.reshape(KB, depth, BY, CX)
+            for piece in range(KB):
+                back[view * KB + piece, :, 8 : 8 + BY] = result[piece]
             return carry
 
-        lax.fori_loop(0, V * KB, block_step, 0)
+        lax.fori_loop(0, V, backward_view, 0)
 
         def spread_view(view, carry):
             edge = None
@@ -376,15 +416,22 @@
     halo_planes = {-1: W, 0: depth, 1: W}
     halo_rows = {-1: 16, 0: height, 1: 16}
     return_rows = {-1: 8, 0: padded, 1: 8}
-    smem = pl.BlockSpec(memory_space=pltpu.SMEM)
-    vmem = pl.BlockSpec(memory_space=pltpu.VMEM)
+    anywhere = pl.BlockSpec(memory_space=pl.ANY)
     count = len(DIRECTIONS)
     return pl.pallas_call(
         functools.partial(kernel, slabs, bricks),
         out_shape=jax.ShapeDtypeStruct((depth, height, width), jnp.float32),
-        in_specs=[smem] * 6 + [vmem, pl.BlockSpec(memory_space=pl.ANY)],
-        out_specs=vmem,
+        in_specs=[anywhere] * 8,
+        out_specs=pl.BlockSpec(memory_space=pltpu.VMEM),
         scratch_shapes=[
+            pltpu.SMEM(routes.shape, jnp.int32),
+            pltpu.SMEM(offsets.shape, jnp.int32),
+            pltpu.SMEM(depth_taps.shape, jnp.float32),
+            pltpu.SMEM(row_taps.shape, jnp.float32),
+            pltpu.SMEM(column_taps.shape, jnp.float32),
+            pltpu.SMEM(background.shape, jnp.float32),
+            pltpu.VMEM((depth, height, width), jnp.float32),
+            pltpu.SemaphoreType.DMA((7,)),
             pltpu.VMEM((bricks, capacity, depth, BY, width), jnp.float32),
             pltpu.VMEM((bricks, capacity, depth, BY, width), jnp.int16),
             pltpu.VMEM((bricks, capacity, depth, BY, width), jnp.int16),
@@ -392,6 +439,7 @@
             pltpu.VMEM((ITERS, depth, height, width), jnp.bfloat16),
             pltpu.VMEM((depth + 2 * W, padded, width), jnp.float32),
             pltpu.VMEM((V, depth, padded, width), jnp.float32),
+            pltpu.VMEM((V, KB * depth * BY, width), jnp.float32),
             pltpu.VMEM((V * KB, depth, BY + 16, width), jnp.float32),
             pltpu.VMEM((V, depth, padded, width), jnp.float32),
             pltpu.VMEM((ITERS, depth + 2 * W, padded, width), jnp.float32),
@@ -416,7 +464,7 @@
             pltpu.SemaphoreType.DMA((ITERS, count)),
         ],
         compiler_params=pltpu.CompilerParams(
-            collective_id=0, has_side_effects=True, vmem_limit_bytes=48 * 2**20
+            collective_id=0, has_side_effects=True, vmem_limit_bytes=62 * 2**20
         ),
     )(routes, offsets, depth_taps, row_taps, column_taps, background, estimate, stored)
 

time: 69.7 us -> 51.8 us (0.74)
  Pallas kernels: 61.7 us -> 49.9 us
  local copies, waits for them, and re-layouts: 7.63 us -> 1.67 us
    pallas_call x1, Pallas kernels: 61.7 us -> 49.9 us  [local(): pl.pallas_call(functools.partial(kernel, slabs, bricks), out_shape=jax.Sh...]
    unnamed x17 -> x1, local copies, waits for them, and re-layouts: 7.63 us -> 1.67 us
where the time goes in v2:
time: 51.8 us; the launch traced here: 51.6 us
  Pallas kernels  49.9 us (96%)
  local copies, waits for them, and re-layouts  1.67 us (3%)
    pallas_call x1, Pallas kernels, local(): pl.pallas_call(functools.partial(kernel, slabs, bricks), out_shape=jax.Sh...  49.9 us
    unnamed x1, local copies, waits for them, and re-layouts  1.67 us

profile of v2, /device:TPU:4, one launch (start us, length us, event | category | flops | bytes accessed | tf_op | source)
XLA Modules:
  0.0 51.6 jit_solution(948180379676614029)
XLA Ops:
  0.0 49.9 %shard_map.82 = f32[8,64,128]{2,1,0:T(8,128)} custom-call(s32[8,24]{1,0:T(8,128)} %routes_in.1, s32[6,32]{1,0:T(8,128)} %offsets_in.1, f32[6,9]{1,0:T(8,128)} %depth_in.1, f32[6,5]{1,0:T(8,128)} %row_in.1, f32[6,9]{1,0:T(8,128)} %column_in.1, f32[6]{0:T(128)} %background_in.1, f32[8,64,128]{2,1,0:T(8,128)} %estimate_in.1, f32[8,6,8,16,128]{4,3,2,1,0:T(8,128)} %bitcast.1), custom_call_target="tpu_custom_call" | custom-call | tf_op jit(solution)/shard_map/pallas_call | solution.py:421
  50.0 1.7 %copy.10 = f32[8,64,128]{2,1,0:T(8,128)} copy(f32[8,64,128]{2,1,0:T(8,128)} %shard_map.82) | data formatting | bytes 524288

commit v3 on v2

--- a/solution.py
+++ b/solution.py
@@ -20,6 +20,8 @@
 TX = 2 * RX + 1
 MIDDLE = 1.25
 SCALE = 43680.0
+ROOT_SCALE = 5900.0
+ROOT_ZERO = 32768.0
 DIRECTIONS = [(dz, db) for dz in (-1, 0, 1) for db in (-1, 0, 1) if (dz, db) != (0, 0)]
 MESH = pl.DeviceIdType.MESH
 
@@ -48,7 +50,6 @@
     coded,
     received,
     slots,
-    rounded,
     extended,
     zblur,
     level,
@@ -61,6 +62,8 @@
     scales,
     halos,
     returns,
+    halos_out,
+    returns_out,
     load_sem,
     data_send,
     data_recv,
@@ -105,8 +108,18 @@
             (there_slab >= 0) & (there_slab < slabs) & (there_brick >= 0) & (there_brick < bricks)
         )
 
-    for buffer in tuple(halos) + tuple(returns):
+    for buffer in halos:
         buffer[...] = jnp.zeros_like(buffer)
+    for buffer in returns:
+        buffer[...] = jnp.full(buffer.shape, -int(ROOT_ZERO), jnp.int32).astype(jnp.int16)
+
+    def pack_halos(sweep, cells):
+        for index, (dz, db) in enumerate(DIRECTIONS):
+            planes = {-1: (0, W), 0: (0, depth), 1: (depth - W, depth)}[dz]
+            rows = {-1: (0, W), 0: (0, height), 1: (height - W, height)}[db]
+            halos_out[index][sweep] = jnp.concatenate(
+                [cells[z, rows[0] : rows[1]] for z in range(*planes)], axis=0
+            ).astype(jnp.bfloat16)
 
     barrier = pltpu.get_barrier_semaphore()
     for step in range(1, bricks):
@@ -130,15 +143,13 @@
         expected = expected + present(dz, db).astype(jnp.int32)
     small[0].wait()
     estimate_now = estimate[...]
-    rounded[0] = estimate_now.astype(jnp.bfloat16)
+    pack_halos(0, estimate_now)
     pl.semaphore_wait(barrier, expected)
 
     def halo_copy(sweep, index):
         dz, db = DIRECTIONS[index]
-        planes = {-1: pl.ds(0, W), 0: pl.ds(0, depth), 1: pl.ds(depth - W, W)}[dz]
-        rows = {-1: pl.ds(0, 16), 0: pl.ds(0, height), 1: pl.ds(height - 16, 16)}[db]
         return pltpu.make_async_remote_copy(
-            src_ref=rounded.at[sweep, planes, rows],
+            src_ref=halos_out[index].at[sweep],
             dst_ref=halos[index].at[sweep],
             send_sem=halo_send.at[sweep, index],
             recv_sem=halo_recv.at[sweep, index],
@@ -148,16 +159,25 @@
 
     def return_copy(sweep, index):
         dz, db = DIRECTIONS[index]
-        planes = {-1: pl.ds(0, W), 0: pl.ds(W, depth), 1: pl.ds(depth + W, W)}[dz]
-        rows = {-1: pl.ds(0, 8), 0: pl.ds(0, padded), 1: pl.ds(padded - 8, 8)}[db]
         return pltpu.make_async_remote_copy(
-            src_ref=correction.at[sweep, planes, rows],
+            src_ref=returns_out[index].at[sweep],
             dst_ref=returns[index].at[sweep],
             send_sem=return_send.at[sweep, index],
             recv_sem=return_recv.at[sweep, index],
             device_id=(slab + dz, brick + db),
             device_id_type=MESH,
         )
+
+    def pack_returns(sweep):
+        for index, (dz, db) in enumerate(DIRECTIONS):
+            planes = {-1: (0, W), 0: (W, W + depth), 1: (W + depth, 2 * W + depth)}[dz]
+            rows = {-1: (0, W), 0: (W, W + height), 1: (W + height, padded)}[db]
+            piece = jnp.concatenate(
+                [correction[sweep, z, rows[0] : rows[1]] for z in range(*planes)], axis=0
+            )
+            root = jnp.sqrt(jnp.maximum(piece, 1e-12))
+            code = jnp.round(root * ROOT_SCALE - ROOT_ZERO).astype(jnp.int32)
+            returns_out[index][sweep] = code.astype(jnp.int16)
 
     def send_all(copy, sweep):
         for index, (dz, db) in enumerate(DIRECTIONS):
@@ -270,16 +290,19 @@
 
     for sweep in range(ITERS):
         if sweep > 0:
-            rounded[sweep] = estimate_now.astype(jnp.bfloat16)
+            pack_halos(sweep, estimate_now)
             send_all(halo_copy, sweep)
-        extended[W : W + depth, W : W + height] = rounded[sweep].astype(jnp.float32)
+        extended[W : W + depth, W : W + height] = estimate_now.astype(jnp.bfloat16).astype(
+            jnp.float32
+        )
         receive_all(halo_copy, sweep)
         for index, (dz, db) in enumerate(DIRECTIONS):
             planes = {1: (0, W), 0: (W, W + depth), -1: (W + depth, 2 * W + depth)}[dz]
             rows = {1: (0, W), 0: (W, W + height), -1: (W + height, padded)}[db]
-            taken = {1: (16 - W, 16), 0: (0, height), -1: (0, W)}[db]
             block = halos[index][sweep].astype(jnp.float32)
-            extended[planes[0] : planes[1], rows[0] : rows[1]] = block[:, taken[0] : taken[1]]
+            size = rows[1] - rows[0]
+            for place, z in enumerate(range(*planes)):
+                extended[z, rows[0] : rows[1]] = block[place * size : (place + 1) * size]
 
         def blur_tile(tile, carry):
             start = pl.multiple_of(tile * 8, 8)
@@ -382,16 +405,19 @@
 
         lax.fori_loop(0, tiles, deep_tile, 0)
 
+        pack_returns(sweep)
         send_all(return_copy, sweep)
         total[...] = correction[sweep, W : W + depth, W : W + height]
         receive_all(return_copy, sweep)
         for index, (dz, db) in enumerate(DIRECTIONS):
             planes = {1: (0, W), 0: (0, depth), -1: (depth - W, depth)}[dz]
             rows = {1: (0, W), 0: (0, height), -1: (height - W, height)}[db]
-            taken = {1: (8 - W, 8), 0: (W, W + height), -1: (0, W)}[db]
-            total[planes[0] : planes[1], rows[0] : rows[1]] += returns[index][
-                sweep, :, taken[0] : taken[1]
-            ]
+            code = returns[index][sweep].astype(jnp.int32).astype(jnp.float32)
+            root = (code + ROOT_ZERO) * (1.0 / ROOT_SCALE)
+            piece = root * root
+            size = rows[1] - rows[0]
+            for place, z in enumerate(range(*planes)):
+                total[z, rows[0] : rows[1]] += piece[place * size : (place + 1) * size]
         if sweep + 1 < ITERS:
             estimate_now = estimate_now * (total[...] / V)
         else:
@@ -414,8 +440,14 @@
     capacity = stored.shape[1]
     padded = height + 2 * W
     halo_planes = {-1: W, 0: depth, 1: W}
-    halo_rows = {-1: 16, 0: height, 1: 16}
-    return_rows = {-1: 8, 0: padded, 1: 8}
+    halo_rows = {-1: W, 0: height, 1: W}
+
+    def faces(dtype):
+        return [
+            pltpu.VMEM((ITERS, halo_planes[dz] * halo_rows[db], width), dtype)
+            for dz, db in DIRECTIONS
+        ]
+
     anywhere = pl.BlockSpec(memory_space=pl.ANY)
     count = len(DIRECTIONS)
     return pl.pallas_call(
@@ -436,7 +468,6 @@
             pltpu.VMEM((bricks, capacity, depth, BY, width), jnp.int16),
             pltpu.VMEM((bricks, capacity, depth, BY, width), jnp.int16),
             pltpu.SMEM((V * KB,), jnp.int32),
-            pltpu.VMEM((ITERS, depth, height, width), jnp.bfloat16),
             pltpu.VMEM((depth + 2 * W, padded, width), jnp.float32),
             pltpu.VMEM((V, depth, padded, width), jnp.float32),
             pltpu.VMEM((V, KB * depth * BY, width), jnp.float32),
@@ -447,14 +478,10 @@
             pltpu.VMEM((V, 2 * CX, CX), jnp.bfloat16),
             pltpu.VMEM((V, CX, CX), jnp.bfloat16),
             pltpu.VMEM((V, 8, CX), jnp.float32),
-            [
-                pltpu.VMEM((ITERS, halo_planes[dz], halo_rows[db], width), jnp.bfloat16)
-                for dz, db in DIRECTIONS
-            ],
-            [
-                pltpu.VMEM((ITERS, halo_planes[dz], return_rows[db], width), jnp.float32)
-                for dz, db in DIRECTIONS
-            ],
+            faces(jnp.bfloat16),
+            faces(jnp.int16),
+            faces(jnp.bfloat16),
+            faces(jnp.int16),
             pltpu.SemaphoreType.DMA((bricks,)),
             pltpu.SemaphoreType.DMA((bricks,)),
             pltpu.SemaphoreType.DMA((bricks,)),

time: 51.8 us -> 47.5 us (0.917)
  Pallas kernels: 49.9 us -> 45.7 us
    pallas_call x1, Pallas kernels: 49.9 us -> 45.7 us  [local(): pl.pallas_call(functools.partial(kernel, slabs, bricks), out_shape=jax.Sh...]
where the time goes in v3:
time: 47.5 us; the launch traced here: 47.3 us
  Pallas kernels  45.7 us (96%)
  local copies, waits for them, and re-layouts  1.67 us (4%)
    pallas_call x1, Pallas kernels, local(): pl.pallas_call(functools.partial(kernel, slabs, bricks), out_shape=jax.Sh...  45.7 us
    unnamed x1, local copies, waits for them, and re-layouts  1.67 us

profile of v3, /device:TPU:4, one launch (start us, length us, event | category | flops | bytes accessed | tf_op | source)
XLA Modules:
  0.0 47.3 jit_solution(4979490322897490427)
XLA Ops:
  0.0 45.7 %shard_map.82 = f32[8,64,128]{2,1,0:T(8,128)} custom-call(s32[8,24]{1,0:T(8,128)} %routes_in.1, s32[6,32]{1,0:T(8,128)} %offsets_in.1, f32[6,9]{1,0:T(8,128)} %depth_in.1, f32[6,5]{1,0:T(8,128)} %row_in.1, f32[6,9]{1,0:T(8,128)} %column_in.1, f32[6]{0:T(128)} %background_in.1, f32[8,64,128]{2,1,0:T(8,128)} %estimate_in.1, f32[8,6,8,16,128]{4,3,2,1,0:T(8,128)} %bitcast.1), custom_call_target="tpu_custom_call" | custom-call | tf_op jit(solution)/shard_map/pallas_call | solution.py:453
  45.7 1.7 %copy.10 = f32[8,64,128]{2,1,0:T(8,128)} copy(f32[8,64,128]{2,1,0:T(8,128)} %shard_map.82) | data formatting | bytes 524288

commit v4 on v3

--- a/solution.py
+++ b/solution.py
@@ -98,8 +98,20 @@
     ]
     for copy in small:
         copy.start()
-    for step in range(1, bricks + 1):
-        load_copy(lax.rem(brick + step, bricks)).start()
+    wide = max(1, round((bricks // 2) ** 0.5))
+    if wide * wide * 2 != bricks:
+        wide = bricks // 2
+    high_count = bricks // 2 // wide
+
+    def partner(step):
+        shift = bricks - 1 - step
+        chip = brick // 2
+        row = (chip // wide + shift // 2 // wide) % high_count
+        column = (chip % wide + shift // 2 % wide) % wide
+        return (row * wide + column) * 2 + (brick % 2 + shift % 2) % 2
+
+    for step in range(bricks):
+        load_copy(partner(step)).start()
 
     def present(dz, db):
         there_slab = slab + dz
@@ -144,7 +156,6 @@
     small[0].wait()
     estimate_now = estimate[...]
     pack_halos(0, estimate_now)
-    pl.semaphore_wait(barrier, expected)
 
     def halo_copy(sweep, index):
         dz, db = DIRECTIONS[index]
@@ -213,10 +224,8 @@
     def encode(cells):
         return jnp.round((cells - MIDDLE) * SCALE).astype(jnp.int32).astype(jnp.int16)
 
-    send_all(halo_copy, 0)
-
-    def send_step(step, carry):
-        target = lax.rem(brick + step, bricks)
+    def code_step(step, carry):
+        target = partner(step)
         load_copy(target).wait()
 
         def code_slot(slot, inner):
@@ -224,10 +233,13 @@
             return inner
 
         lax.fori_loop(0, capacity, code_slot, 0)
-        data_copy(target, brick).start()
         return carry
 
-    lax.fori_loop(1, bricks, send_step, 0)
+    lax.fori_loop(0, bricks - 1, code_step, 0)
+    pl.semaphore_wait(barrier, expected)
+    send_all(halo_copy, 0)
+    for step in range(bricks - 1):
+        data_copy(partner(step), brick).start()
     load_copy(brick).wait()
 
     def code_own(slot, carry):

time: 47.5 us -> 48.2 us (1.015)
  the two profiles are of different devices: /device:TPU:4 before, /device:TPU:0 now
where the time goes in v4:
time: 48.2 us; the launch traced here: 48.1 us
  Pallas kernels  46.4 us (96%)
  local copies, waits for them, and re-layouts  1.67 us (3%)
    pallas_call x1, Pallas kernels, local(): pl.pallas_call(functools.partial(kernel, slabs, bricks), out_shape=jax.Sh...  46.4 us
    unnamed x1, local copies, waits for them, and re-layouts  1.67 us

profile of v4, /device:TPU:0, one launch (start us, length us, event | category | flops | bytes accessed | tf_op | source)
XLA Modules:
  0.0 48.1 jit_solution(7471792721222364278)
XLA Ops:
  0.0 46.4 %shard_map.82 = f32[8,64,128]{2,1,0:T(8,128)} custom-call(s32[8,24]{1,0:T(8,128)} %routes_in.1, s32[6,32]{1,0:T(8,128)} %offsets_in.1, f32[6,9]{1,0:T(8,128)} %depth_in.1, f32[6,5]{1,0:T(8,128)} %row_in.1, f32[6,9]{1,0:T(8,128)} %column_in.1, f32[6]{0:T(128)} %background_in.1, f32[8,64,128]{2,1,0:T(8,128)} %estimate_in.1, f32[8,6,8,16,128]{4,3,2,1,0:T(8,128)} %bitcast.1), custom_call_target="tpu_custom_call" | custom-call | tf_op jit(solution)/shard_map/pallas_call | solution.py:465
  46.4 1.7 %copy.10 = f32[8,64,128]{2,1,0:T(8,128)} copy(f32[8,64,128]{2,1,0:T(8,128)} %shard_map.82) | data formatting | bytes 524288
